TPU v7x, 512 devices: a whole 4x4x16 slice. The times are simulated.
512 devices in a mesh: dp: 64 (over y, z), mp: 8 (over x, core).
Axes of the slice: x: 4, y: 4, z: 16, core: 2. Of those that a mesh axis runs over, the one named last changes fastest.
Arguments:
- q_gen: bfloat16 [64, 512, 4096], P('mp', 'dp'), may hold values from -300 to 300
- k_gen: bfloat16 [64, 512, 1024], P('mp', 'dp'), may hold values from -9 to 9
- v_gen: bfloat16 [64, 512, 1024], P('mp', 'dp'), may hold values from -6 to 6
- grad_gen: bfloat16 [64, 512, 4096], P('mp', 'dp'), may hold values from -6 to 6
- lengths: int32 [64], replicated, may hold values from 16 to 512, as said below
- swap_flags: int32 [2, 64], replicated, may hold values from 0 to 1, as said below
Outputs:
- attn_out: bfloat16 [64, 512, 4096], P('dp', None, 'mp')
- grad_q: bfloat16 [64, 512, 4096], P('dp', None, 'mp')
- grad_k: bfloat16 [64, 512, 1024], P('dp', None, 'mp')
- grad_v: bfloat16 [64, 512, 1024], P('dp', None, 'mp')
Inputs may be any that keep to these rules, and one draw needn't show every extreme that they name: `lengths`: some rollout has exactly 512 tokens. swap_flags[r, d] == swap_flags[r, d XOR (64 / 2^(r+1))]; device 64 - 1 swaps in every round.
All inputs are finite; a program needn't handle non-finite values.
Results may differ from a plain program's by a relative error of at most 0.005.
Values may be sent and summed in bfloat16 or wider, within the bound.
A program may use at most 64 MiB of HBM per device.

v0:
```python
import math

import jax
import jax.numpy as jnp
from jax import lax
from jax.sharding import PartitionSpec as P

HEAD = 128


def partner_2(block, axis, distance):
    count = lax.axis_size(axis)
    route = []
    for low in range(count):
        high = low | 1 << distance
        if high != low and high < count:
            route += [(low, high), (high, low)]
    return lax.ppermute(block, axis, route)


def one_head(q_head, k_head, v_head, grad_head, length):
    rows_seq = q_head.shape[0]
    inv_root = 1.0 / math.sqrt(q_head.shape[1])
    scores = jnp.dot(q_head, k_head.T, preferred_element_type=jnp.float32) * inv_root
    position = jnp.arange(rows_seq)
    visible = (position[None, :] <= position[:, None]) & (position[None, :] < length)
    scores = jnp.where(visible, scores, -1e30)
    row_max = jnp.max(scores, axis=-1, keepdims=True)
    weights = jnp.exp(scores - row_max)
    weights = weights / jnp.sum(weights, axis=-1, keepdims=True)
    probs = weights.astype(jnp.bfloat16)
    live_rows = (position < length)[:, None]
    out_head = jnp.where(live_rows, jnp.dot(probs, v_head, preferred_element_type=jnp.float32), 0.0)
    live_grad = jnp.where(live_rows, grad_head, jnp.zeros_like(grad_head))
    dv_head = jnp.dot(probs.T, live_grad, preferred_element_type=jnp.float32)
    dprob = jnp.dot(live_grad, v_head.T, preferred_element_type=jnp.float32)
    row_delta = jnp.sum(weights * dprob, axis=-1, keepdims=True)
    dscore = (weights * (dprob - row_delta) * inv_root).astype(jnp.bfloat16)
    dq_head = jnp.dot(dscore, k_head, preferred_element_type=jnp.float32)
    dk_head = jnp.dot(dscore.T, q_head, preferred_element_type=jnp.float32)
    return (out_head, dq_head, dk_head, dv_head)


def attend_sequence(queries, keys, values, grads, length, kv_heads):
    rows_seq = queries.shape[0]
    head_dim = keys.shape[1] // kv_heads
    q_heads = queries.shape[1] // head_dim
    per_group = q_heads // kv_heads
    q_split = queries.reshape(rows_seq, q_heads, head_dim).transpose(1, 0, 2)
    g_split = grads.reshape(rows_seq, q_heads, head_dim).transpose(1, 0, 2)
    k_split = jnp.repeat(
        keys.reshape(rows_seq, kv_heads, head_dim).transpose(1, 0, 2), per_group, axis=0
    )
    v_split = jnp.repeat(
        values.reshape(rows_seq, kv_heads, head_dim).transpose(1, 0, 2), per_group, axis=0
    )

    def run_head(items):
        return one_head(items[0], items[1], items[2], items[3], length)

    outs, dqs, dks, dvs = lax.map(run_head, (q_split, k_split, v_split, g_split))
    out_rows = outs.transpose(1, 0, 2).reshape(rows_seq, q_heads * head_dim).astype(jnp.bfloat16)
    dq_rows = dqs.transpose(1, 0, 2).reshape(rows_seq, q_heads * head_dim).astype(jnp.bfloat16)
    dk_rows = dks.reshape(kv_heads, per_group, rows_seq, head_dim).sum(axis=1)
    dk_rows = dk_rows.transpose(1, 0, 2).reshape(rows_seq, kv_heads * head_dim).astype(jnp.bfloat16)
    dv_rows = dvs.reshape(kv_heads, per_group, rows_seq, head_dim).sum(axis=1)
    dv_rows = dv_rows.transpose(1, 0, 2).reshape(rows_seq, kv_heads * head_dim).astype(jnp.bfloat16)
    return (out_rows, dq_rows, dk_rows, dv_rows)


def place_sequences(swap_flags, devices):
    slot_ids = jnp.arange(devices, dtype=jnp.int32)
    slot_seq = slot_ids
    for round_index in range(swap_flags.shape[0]):
        partner = jnp.bitwise_xor(slot_ids, devices >> round_index + 1)
        slot_seq = jnp.where(swap_flags[round_index] == 1, slot_seq[partner], slot_seq)
    return slot_seq


def shards(q_gen, k_gen, v_gen, grad_gen, lengths, swap_flags):
    devices = lax.axis_size("dp")
    my_index = lax.axis_index("dp")
    rounds_all = swap_flags.shape[0]
    slot_seq = place_sequences(swap_flags, devices)
    queries, keys, values, grads = (
        lax.all_to_all(q_gen, "mp", split_axis=2, concat_axis=0, tiled=True),
        lax.all_to_all(k_gen, "mp", split_axis=2, concat_axis=0, tiled=True),
        lax.all_to_all(v_gen, "mp", split_axis=2, concat_axis=0, tiled=True),
        lax.all_to_all(grad_gen, "mp", split_axis=2, concat_axis=0, tiled=True),
    )
    queries, keys, values, grads = (
        lax.all_to_all(queries, "dp", split_axis=0, concat_axis=1, tiled=True),
        lax.all_to_all(keys, "dp", split_axis=0, concat_axis=1, tiled=True),
        lax.all_to_all(values, "dp", split_axis=0, concat_axis=1, tiled=True),
        lax.all_to_all(grads, "dp", split_axis=0, concat_axis=1, tiled=True),
    )
    for round_index in range(rounds_all):
        bit_place = devices.bit_length() - 2 - round_index
        swapped = swap_flags[round_index, my_index] == 1
        received = partner_2((queries, keys, values, grads), "dp", bit_place)
        queries = jnp.where(swapped, received[0], queries)
        keys = jnp.where(swapped, received[1], keys)
        values = jnp.where(swapped, received[2], values)
        grads = jnp.where(swapped, received[3], grads)
    length = lengths[slot_seq[my_index]]
    kv_heads = keys.shape[2] // HEAD
    out_rows, dq_rows, dk_rows, dv_rows = attend_sequence(
        queries[0], keys[0], values[0], grads[0], length, kv_heads
    )
    return (out_rows[None], dq_rows[None], dk_rows[None], dv_rows[None])


def solution(mesh):
    in_specs = (
        P("mp", "dp", None),
        P("mp", "dp", None),
        P("mp", "dp", None),
        P("mp", "dp", None),
        P(),
        P(),
    )
    out_specs = (P("dp", None, "mp"), P("dp", None, "mp"), P("dp", None, "mp"), P("dp", None, "mp"))
    return jax.shard_map(shards, mesh=mesh, in_specs=in_specs, out_specs=out_specs, check_vma=False)
```

profile of v0, /device:TPU:40, one launch (start us, length us, event | category | flops | bytes accessed | tf_op | source)
XLA Modules:
  0.0 299.8 jit_solution(222468088917307788)
XLA Ops:
  3.0 2.8 reshape.150
  5.9 4.3 %all-to-all-start.2 = ((bf16[8,2,4096]{2,1,0:T(2,128)(2,1)}), bf16[8,2,4096]{2,1,0:T(2,128)(2,1)S(1)}, u32[]{:S(2)}, u32[]{:S(2)}) async-start(bf16[8,2,4096]{2,1,0:T(2,128)(2,1)} %reshape.150), calls=%async_computation.2 | async-start | bytes 262144 | tf_op jit(solution)/shard_map/all_to_all | solution.py:87
  12.5 2.8 reshape.152
  16.3 3.8 %all-to-all-start.4 = ((bf16[8,2,4096]{2,1,0:T(2,128)(2,1)}), bf16[8,2,4096]{2,1,0:T(2,128)(2,1)S(1)}, u32[]{:S(2)}, u32[]{:S(2)}) async-start(bf16[8,2,4096]{2,1,0:T(2,128)(2,1)} %reshape.152), calls=%async_computation.4 | async-start | bytes 262144 | tf_op jit(solution)/shard_map/all_to_all | solution.py:88
  20.2 7.2 %copy.42 = bf16[8,8,4096]{1,0,2:T(8,128)(2,1)} copy(bf16[8,8,4096]{2,1,0:T(8,128)(2,1)S(1)} %copy-done) | data formatting | bytes 1048576 | tf_op args[3]
  27.4 11.2 %reshape.154 = bf16[8,2,16384]{2,1,0:T(2,128)(2,1)} reshape(bf16[4096,8,8]{2,1,0:T(8,128)(2,1)} %bitcast.147) | data formatting | bytes 1048576
  38.5 4.8 %all-to-all-start.6 = ((bf16[8,2,16384]{2,1,0:T(2,128)(2,1)}), bf16[8,2,16384]{2,1,0:T(2,128)(2,1)S(1)}, u32[]{:S(2)}, u32[]{:S(2)}) async-start(bf16[8,2,16384]{2,1,0:T(2,128)(2,1)} %reshape.154), calls=%async_computation.6 | async-start | bytes 1048576 | tf_op jit(solution)/shard_map/all_to_all | solution.py:89
  43.3 7.2 %copy.31 = bf16[8,8,4096]{1,0,2:T(8,128)(2,1)} copy(bf16[8,8,4096]{2,1,0:T(8,128)(2,1)S(1)} %copy-done.1) | data formatting | bytes 1048576 | tf_op args[0]
  50.5 11.2 %reshape.148 = bf16[8,2,16384]{2,1,0:T(2,128)(2,1)} reshape(bf16[4096,8,8]{2,1,0:T(8,128)(2,1)} %bitcast.148) | data formatting | bytes 1048576
  61.6 4.8 %all-to-all-start = ((bf16[8,2,16384]{2,1,0:T(2,128)(2,1)}), bf16[8,2,16384]{2,1,0:T(2,128)(2,1)S(1)}, u32[]{:S(2)}, u32[]{:S(2)}) async-start(bf16[8,2,16384]{2,1,0:T(2,128)(2,1)} %reshape.148), calls=%async_computation | async-start | bytes 1048576 | tf_op jit(solution)/shard_map/all_to_all | solution.py:86
  70.6 6.2 %all-to-all-done = bf16[8,2,16384]{2,1,0:T(2,128)(2,1)S(1)} async-done(((bf16[8,2,16384]{2,1,0:T(2,128)(2,1)}), bf16[8,2,16384]{2,1,0:T(2,128)(2,1)S(1)}, u32[]{:S(2)}, u32[]{:S(2)}) %all-to-all-start) | async-done | bytes 524320 | tf_op jit(solution)/shard_map/all_to_all | solution.py:86
  76.8 18.3 %all-to-all-start.3 = ((bf16[64,8,128]{2,1,0:T(8,128)(2,1)}), bf16[64,8,128]{2,1,0:T(8,128)(2,1)S(1)}, u32[]{:S(2)}, u32[]{:S(2)}) async-start(bf16[64,8,128]{2,1,0:T(8,128)(2,1)} %bitcast.27), calls=%async_computation.3 | async-start | bytes 262144 | tf_op jit(solution)/shard_map/all_to_all | solution.py:93
  99.2 10.7 %all-to-all-done.3 = bf16[64,8,128]{2,1,0:T(8,128)(2,1)S(1)} async-done(((bf16[64,8,128]{2,1,0:T(8,128)(2,1)}), bf16[64,8,128]{2,1,0:T(8,128)(2,1)S(1)}, u32[]{:S(2)}, u32[]{:S(2)}) %all-to-all-start.3) | async-done | bytes 131104 | tf_op jit(solution)/shard_map/all_to_all | solution.py:93
  109.9 6.8 %all-to-all-start.5 = ((bf16[64,8,128]{2,1,0:T(8,128)(2,1)}), bf16[64,8,128]{2,1,0:T(8,128)(2,1)S(1)}, u32[]{:S(2)}, u32[]{:S(2)}) async-start(bf16[64,8,128]{2,1,0:T(8,128)(2,1)} %bitcast.33), calls=%async_computation.5 | async-start | bytes 262144 | tf_op jit(solution)/shard_map/all_to_all | solution.py:94
  116.8 11.0 %reshape.155 = bf16[4096,8,8]{2,1,0:T(8,128)(2,1)} reshape(bf16[8,2,16384]{2,1,0:T(2,128)(2,1)S(1)} %all-to-all-done.6) | data formatting | bytes 1048576
  127.7 9.0 %copy.44 = bf16[8,8,8,512]{3,2,1,0:T(8,128)(2,1)} copy(bf16[8,8,8,512]{2,1,3,0:T(8,128)(2,1)} %bitcast.145) | data formatting | bytes 1048576 | tf_op jit(solution)/shard_map/all_to_all | solution.py:89
  136.7 15.1 %all-to-all-start.7 = ((bf16[64,8,512]{2,1,0:T(8,128)(2,1)}), bf16[64,8,512]{2,1,0:T(8,128)(2,1)S(1)}, u32[]{:S(2)}, u32[]{:S(2)}) async-start(bf16[64,8,512]{2,1,0:T(8,128)(2,1)} %bitcast.39), calls=%async_computation.7 | async-start | bytes 1048576 | tf_op jit(solution)/shard_map/all_to_all | solution.py:95
  151.9 11.0 %reshape.149 = bf16[4096,8,8]{2,1,0:T(8,128)(2,1)} reshape(bf16[8,2,16384]{2,1,0:T(2,128)(2,1)S(1)} %all-to-all-done) | data formatting | bytes 1048576
  162.9 9.0 %copy.33 = bf16[8,8,8,512]{3,2,1,0:T(8,128)(2,1)} copy(bf16[8,8,8,512]{2,1,3,0:T(8,128)(2,1)} %bitcast.146) | data formatting | bytes 1048576 | tf_op jit(solution)/shard_map/all_to_all | solution.py:86
  171.8 10.2 %all-to-all-done.7 = bf16[64,8,512]{2,1,0:T(8,128)(2,1)S(1)} async-done(((bf16[64,8,512]{2,1,0:T(8,128)(2,1)}), bf16[64,8,512]{2,1,0:T(8,128)(2,1)S(1)}, u32[]{:S(2)}, u32[]{:S(2)}) %all-to-all-start.7) | async-done | bytes 524320 | tf_op jit(solution)/shard_map/all_to_all | solution.py:95
  182.1 7.1 %all-to-all-start.1 = ((bf16[64,8,512]{2,1,0:T(8,128)(2,1)}), bf16[64,8,512]{2,1,0:T(8,128)(2,1)S(1)}, u32[]{:S(2)}, u32[]{:S(2)}) async-start(bf16[64,8,512]{2,1,0:T(8,128)(2,1)} %bitcast.20), calls=%async_computation.1 | async-start | bytes 1048576 | tf_op jit(solution)/shard_map/all_to_all | solution.py:92
  190.8 4.2 %collective-permute-start.2 = (bf16[1,512,128]{2,1,0:T(8,128)(2,1)S(1)}, bf16[1,512,128]{2,1,0:T(8,128)(2,1)S(1)}, u32[]{:S(2)}, u32[]{:S(2)}) collective-permute-start(bf16[1,512,128]{2,1,0:T(8,128)(2,1)S(1)} %bitcast.158), channel_id=1, source_target_pairs={{0,256},{256,0},{8,264},{264,8},{16,272},{272,16},{24,280},{280,24... | collective-permute-start | bytes 393224 | tf_op jit(solution)/shard_map/ppermute | solution.py:18
  195.2 3.2 %collective-permute-start.6 = (bf16[1,512,512]{1,2,0:T(8,128)(2,1)S(1)}, bf16[1,512,512]{1,2,0:T(8,128)(2,1)S(1)}, u32[]{:S(2)}, u32[]{:S(2)}) collective-permute-start(bf16[1,512,512]{1,2,0:T(8,128)(2,1)S(1)} %copy.45), channel_id=1, source_target_pairs={{0,256},{256,0},{8,264},{264,8},{16,272},{272,16},{24,280},{280,24... | collective-permute-start | bytes 1572872 | tf_op jit(solution)/shard_map/ppermute | solution.py:18
  203.3 4.2 %collective-permute-start.4 = (bf16[1,512,128]{2,1,0:T(8,128)(2,1)S(1)}, bf16[1,512,128]{2,1,0:T(8,128)(2,1)S(1)}, u32[]{:S(2)}, u32[]{:S(2)}) collective-permute-start(bf16[1,512,128]{2,1,0:T(8,128)(2,1)S(1)} %bitcast.159), channel_id=1, source_target_pairs={{0,256},{256,0},{8,264},{264,8},{16,272},{272,16},{24,280},{280,24... | collective-permute-start | bytes 393224 | tf_op jit(solution)/shard_map/ppermute | solution.py:18
  207.4 12.4 %all-to-all-done.1 = bf16[64,8,512]{2,1,0:T(8,128)(2,1)S(1)} async-done(((bf16[64,8,512]{2,1,0:T(8,128)(2,1)}), bf16[64,8,512]{2,1,0:T(8,128)(2,1)S(1)}, u32[]{:S(2)}, u32[]{:S(2)}) %all-to-all-start.1) | async-done | bytes 524320 | tf_op jit(solution)/shard_map/all_to_all | solution.py:92
  220.0 4.2 %collective-permute-start = (bf16[1,512,512]{1,2,0:T(8,128)(2,1)S(1)}, bf16[1,512,512]{1,2,0:T(8,128)(2,1)S(1)}, u32[]{:S(2)}, u32[]{:S(2)}) collective-permute-start(bf16[1,512,512]{1,2,0:T(8,128)(2,1)S(1)} %copy.34), channel_id=1, source_target_pairs={{0,256},{256,0},{8,264},{264,8},{16,272},{272,16},{24,280},{280,24... | collective-permute-start | bytes 1572872 | tf_op jit(solution)/shard_map/ppermute | solution.py:18
  224.3 3.3 %collective-permute-start.3 = (bf16[1,512,128]{2,1,0:T(8,128)(2,1)S(1)}, bf16[1,512,128]{2,1,0:T(8,128)(2,1)S(1)}, u32[]{:S(2)}, u32[]{:S(2)}) collective-permute-start(bf16[1,512,128]{2,1,0:T(8,128)(2,1)S(1)} %broadcast_select_fusion.5), channel_id=1, source_target_pairs={{0,128},{128,0},{8,136},{136,8},{16,144},{144,16},{24,152},{152,24... | collective-permute-start | bytes 393224 | tf_op jit(solution)/shard_map/ppermute | solution.py:18
  230.2 3.3 %collective-permute-start.7 = (bf16[1,512,512]{1,2,0:T(8,128)(2,1)S(1)}, bf16[1,512,512]{1,2,0:T(8,128)(2,1)S(1)}, u32[]{:S(2)}, u32[]{:S(2)}) collective-permute-start(bf16[1,512,512]{1,2,0:T(8,128)(2,1)S(1)} %broadcast_select_fusion), channel_id=1, source_target_pairs={{0,128},{128,0},{8,136},{136,8},{16,144},{144,16},{24,152},{152,24... | collective-permute-start | bytes 1572872 | tf_op jit(solution)/shard_map/ppermute | solution.py:18
  233.5 4.8 %collective-permute-done = bf16[1,512,512]{1,2,0:T(8,128)(2,1)S(1)} collective-permute-done((bf16[1,512,512]{1,2,0:T(8,128)(2,1)S(1)}, bf16[1,512,512]{1,2,0:T(8,128)(2,1)S(1)}, u32[]{:S(2)}, u32[]{:S(2)}) %collective-permute-start) | collective-permute-done | bytes 524320 | tf_op jit(solution)/shard_map/ppermute | solution.py:18
  244.0 11.2 %collective-permute-done.7 = bf16[1,512,512]{1,2,0:T(8,128)(2,1)S(1)} collective-permute-done((bf16[1,512,512]{1,2,0:T(8,128)(2,1)S(1)}, bf16[1,512,512]{1,2,0:T(8,128)(2,1)S(1)}, u32[]{:S(2)}, u32[]{:S(2)}) %collective-permute-start.7) | collective-permute-done | bytes 524320 | tf_op jit(solution)/shard_map/ppermute | solution.py:18
  255.3 9.8 %collective-permute-done.1 = bf16[1,512,512]{1,2,0:T(8,128)(2,1)S(1)} collective-permute-done((bf16[1,512,512]{1,2,0:T(8,128)(2,1)S(1)}, bf16[1,512,512]{1,2,0:T(8,128)(2,1)S(1)}, u32[]{:S(2)}, u32[]{:S(2)}) %collective-permute-start.1) | collective-permute-done | bytes 524320 | tf_op jit(solution)/shard_map/ppermute | solution.py:18
  265.3 25.7 %while.16 = (s32[]{:T(128)}, bf16[4,512,128]{2,1,0:T(8,128)(2,1)}, bf16[4,512,128]{2,1,0:T(8,128)(2,1)}, f32[4,512,128]{2,1,0:T(8,128)}, f32[4,512,128]{2,1,0:T(...) while((s32[]{:T(128)}, bf16[4,512,128]{2,1,0:T(8,128)(2,1)}, ...), condition=%wide.region_4.5_spmd, body=%wide.region_0.4_spmd.sunk | while | flops 408878080 | bytes 16811184 | solution.py:61
  (119 shorter events, 60.8 us)
Async XLA Ops:
  0.6 19.5 %copy-start = (bf16[8,8,4096]{2,1,0:T(8,128)(2,1)S(1)}, bf16[8,8,4096]{2,1,0:T(8,128)(2,1)}, u32[]{:S(2)}) copy-start(bf16[8,8,4096]{2,1,0:T(8,128)(2,1)} %param.11) | copy-start | bytes 1572868
  5.9 10.4 %all-to-all-start.2 = ((bf16[8,2,4096]{2,1,0:T(2,128)(2,1)}), bf16[8,2,4096]{2,1,0:T(2,128)(2,1)S(1)}, u32[]{:S(2)}, u32[]{:S(2)}) async-start(bf16[8,2,4096]{2,1,0:T(2,128)(2,1)} %reshape.150), calls=%async_computation.2 | async-start | bytes 262144 | tf_op jit(solution)/shard_map/all_to_all | solution.py:87
  16.3 22.2 %all-to-all-start.4 = ((bf16[8,2,4096]{2,1,0:T(2,128)(2,1)}), bf16[8,2,4096]{2,1,0:T(2,128)(2,1)S(1)}, u32[]{:S(2)}, u32[]{:S(2)}) async-start(bf16[8,2,4096]{2,1,0:T(2,128)(2,1)} %reshape.152), calls=%async_computation.4 | async-start | bytes 262144 | tf_op jit(solution)/shard_map/all_to_all | solution.py:88
  20.2 23.1 %copy-start.1 = (bf16[8,8,4096]{2,1,0:T(8,128)(2,1)S(1)}, bf16[8,8,4096]{2,1,0:T(8,128)(2,1)}, u32[]{:S(2)}) copy-start(bf16[8,8,4096]{2,1,0:T(8,128)(2,1)} %param.8) | copy-start | bytes 1572868
  38.5 23.1 %all-to-all-start.6 = ((bf16[8,2,16384]{2,1,0:T(2,128)(2,1)}), bf16[8,2,16384]{2,1,0:T(2,128)(2,1)S(1)}, u32[]{:S(2)}, u32[]{:S(2)}) async-start(bf16[8,2,16384]{2,1,0:T(2,128)(2,1)} %reshape.154), calls=%async_computation.6 | async-start | bytes 1048576 | tf_op jit(solution)/shard_map/all_to_all | solution.py:89
  61.6 15.1 %all-to-all-start = ((bf16[8,2,16384]{2,1,0:T(2,128)(2,1)}), bf16[8,2,16384]{2,1,0:T(2,128)(2,1)S(1)}, u32[]{:S(2)}, u32[]{:S(2)}) async-start(bf16[8,2,16384]{2,1,0:T(2,128)(2,1)} %reshape.148), calls=%async_computation | async-start | bytes 1048576 | tf_op jit(solution)/shard_map/all_to_all | solution.py:86
  76.8 33.2 %all-to-all-start.3 = ((bf16[64,8,128]{2,1,0:T(8,128)(2,1)}), bf16[64,8,128]{2,1,0:T(8,128)(2,1)S(1)}, u32[]{:S(2)}, u32[]{:S(2)}) async-start(bf16[64,8,128]{2,1,0:T(8,128)(2,1)} %bitcast.27), calls=%async_computation.3 | async-start | bytes 262144 | tf_op jit(solution)/shard_map/all_to_all | solution.py:93
  109.9 26.8 %all-to-all-start.5 = ((bf16[64,8,128]{2,1,0:T(8,128)(2,1)}), bf16[64,8,128]{2,1,0:T(8,128)(2,1)S(1)}, u32[]{:S(2)}, u32[]{:S(2)}) async-start(bf16[64,8,128]{2,1,0:T(8,128)(2,1)} %bitcast.33), calls=%async_computation.5 | async-start | bytes 262144 | tf_op jit(solution)/shard_map/all_to_all | solution.py:94
  136.7 45.3 %all-to-all-start.7 = ((bf16[64,8,512]{2,1,0:T(8,128)(2,1)}), bf16[64,8,512]{2,1,0:T(8,128)(2,1)S(1)}, u32[]{:S(2)}, u32[]{:S(2)}) async-start(bf16[64,8,512]{2,1,0:T(8,128)(2,1)} %bitcast.39), calls=%async_computation.7 | async-start | bytes 1048576 | tf_op jit(solution)/shard_map/all_to_all | solution.py:95
  151.9 38.1 %copy-start.4 = (s32[2,64]{1,0:T(2,128)S(1)}, s32[2,64]{1,0:T(2,128)}, u32[]{:S(2)}) copy-start(s32[2,64]{1,0:T(2,128)} %param.13) | copy-start | bytes 1540
  151.9 50.8 %copy-start.5 = (s32[64]{0:T(128)S(1)}, s32[64]{0:T(128)}, u32[]{:S(2)}) copy-start(s32[64]{0:T(128)} %param.12) | copy-start | bytes 772
  182.1 37.7 %all-to-all-start.1 = ((bf16[64,8,512]{2,1,0:T(8,128)(2,1)}), bf16[64,8,512]{2,1,0:T(8,128)(2,1)S(1)}, u32[]{:S(2)}, u32[]{:S(2)}) async-start(bf16[64,8,512]{2,1,0:T(8,128)(2,1)} %bitcast.20), calls=%async_computation.1 | async-start | bytes 1048576 | tf_op jit(solution)/shard_map/all_to_all | solution.py:92
  190.8 33.4 %collective-permute-start.2 = (bf16[1,512,128]{2,1,0:T(8,128)(2,1)S(1)}, bf16[1,512,128]{2,1,0:T(8,128)(2,1)S(1)}, u32[]{:S(2)}, u32[]{:S(2)}) collective-permute-start(bf16[1,512,128]{2,1,0:T(8,128)(2,1)S(1)} %bitcast.158), channel_id=1, source_target_pairs={{0,256},{256,0},{8,264},{264,8},{16,272},{272,16},{24,280},{280,24... | collective-permute-start | bytes 393224 | tf_op jit(solution)/shard_map/ppermute | solution.py:18
  195.2 35.0 %collective-permute-start.6 = (bf16[1,512,512]{1,2,0:T(8,128)(2,1)S(1)}, bf16[1,512,512]{1,2,0:T(8,128)(2,1)S(1)}, u32[]{:S(2)}, u32[]{:S(2)}) collective-permute-start(bf16[1,512,512]{1,2,0:T(8,128)(2,1)S(1)} %copy.45), channel_id=1, source_target_pairs={{0,256},{256,0},{8,264},{264,8},{16,272},{272,16},{24,280},{280,24... | collective-permute-start | bytes 1572872 | tf_op jit(solution)/shard_map/ppermute | solution.py:18
  203.3 24.3 %collective-permute-start.4 = (bf16[1,512,128]{2,1,0:T(8,128)(2,1)S(1)}, bf16[1,512,128]{2,1,0:T(8,128)(2,1)S(1)}, u32[]{:S(2)}, u32[]{:S(2)}) collective-permute-start(bf16[1,512,128]{2,1,0:T(8,128)(2,1)S(1)} %bitcast.159), channel_id=1, source_target_pairs={{0,256},{256,0},{8,264},{264,8},{16,272},{272,16},{24,280},{280,24... | collective-permute-start | bytes 393224 | tf_op jit(solution)/shard_map/ppermute | solution.py:18
  220.0 18.2 %collective-permute-start = (bf16[1,512,512]{1,2,0:T(8,128)(2,1)S(1)}, bf16[1,512,512]{1,2,0:T(8,128)(2,1)S(1)}, u32[]{:S(2)}, u32[]{:S(2)}) collective-permute-start(bf16[1,512,512]{1,2,0:T(8,128)(2,1)S(1)} %copy.34), channel_id=1, source_target_pairs={{0,256},{256,0},{8,264},{264,8},{16,272},{272,16},{24,280},{280,24... | collective-permute-start | bytes 1572872 | tf_op jit(solution)/shard_map/ppermute | solution.py:18
  224.3 16.9 %collective-permute-start.3 = (bf16[1,512,128]{2,1,0:T(8,128)(2,1)S(1)}, bf16[1,512,128]{2,1,0:T(8,128)(2,1)S(1)}, u32[]{:S(2)}, u32[]{:S(2)}) collective-permute-start(bf16[1,512,128]{2,1,0:T(8,128)(2,1)S(1)} %broadcast_select_fusion.5), channel_id=1, source_target_pairs={{0,128},{128,0},{8,136},{136,8},{16,144},{144,16},{24,152},{152,24... | collective-permute-start | bytes 393224 | tf_op jit(solution)/shard_map/ppermute | solution.py:18
  227.6 16.4 %collective-permute-start.5 = (bf16[1,512,128]{2,1,0:T(8,128)(2,1)S(1)}, bf16[1,512,128]{2,1,0:T(8,128)(2,1)S(1)}, u32[]{:S(2)}, u32[]{:S(2)}) collective-permute-start(bf16[1,512,128]{2,1,0:T(8,128)(2,1)S(1)} %broadcast_select_fusion.4), channel_id=1, source_target_pairs={{0,128},{128,0},{8,136},{136,8},{16,144},{144,16},{24,152},{152,24... | collective-permute-start | bytes 393224 | tf_op jit(solution)/shard_map/ppermute | solution.py:18
  230.2 25.0 %collective-permute-start.7 = (bf16[1,512,512]{1,2,0:T(8,128)(2,1)S(1)}, bf16[1,512,512]{1,2,0:T(8,128)(2,1)S(1)}, u32[]{:S(2)}, u32[]{:S(2)}) collective-permute-start(bf16[1,512,512]{1,2,0:T(8,128)(2,1)S(1)} %broadcast_select_fusion), channel_id=1, source_target_pairs={{0,128},{128,0},{8,136},{136,8},{16,144},{144,16},{24,152},{152,24... | collective-permute-start | bytes 1572872 | tf_op jit(solution)/shard_map/ppermute | solution.py:18
  238.3 26.7 %collective-permute-start.1 = (bf16[1,512,512]{1,2,0:T(8,128)(2,1)S(1)}, bf16[1,512,512]{1,2,0:T(8,128)(2,1)S(1)}, u32[]{:S(2)}, u32[]{:S(2)}) collective-permute-start(bf16[1,512,512]{1,2,0:T(8,128)(2,1)S(1)} %broadcast_select_fusion.1), channel_id=1, source_target_pairs={{0,128},{128,0},{8,136},{136,8},{16,144},{144,16},{24,152},{152,24... | collective-permute-start | bytes 1572872 | tf_op jit(solution)/shard_map/ppermute | solution.py:18
  266.6 2.9 copy-start.2
  269.9 0.8 copy-start.3
  273.0 2.9 copy-start.2
  276.3 0.8 copy-start.3
  279.5 2.9 copy-start.2
  282.7 0.8 copy-start.3
  285.9 2.9 copy-start.2
  289.2 0.8 copy-start.3
where the time goes:
time: 302 us; the launch traced here: 300 us
  local copies, waits for them, and re-layouts  108 us (36%)
  starting transfers between devices  92.2 us (31%)
  waiting for transfers between devices  69.5 us (23%)
  matrix products  17.3 us (6%)
  other arithmetic  8.87 us (3%)
  between operations  4.05 us (1%)
    unnamed x20, local copies, waits for them, and re-layouts  73.9 us
    ppermute x8, waiting for transfers between devices, partner_2(): return lax.ppermute(block, axis, route)  29 us
    ppermute x8, starting transfers between devices, partner_2(): return lax.ppermute(block, axis, route)  27.2 us
    all_to_all x1, starting transfers between devices, shards(): lax.all_to_all(keys, 'dp', split_axis=0, concat_axis=1, tiled=True)  18.3 us
    all_to_all x1, starting transfers between devices, shards(): lax.all_to_all(grads, 'dp', split_axis=0, concat_axis=1, tiled=True)  15.1 us
    all_to_all x1, waiting for transfers between devices, shards(): lax.all_to_all(queries, 'dp', split_axis=0, concat_axis=1, tiled=True)  12.4 us
    all_to_all x1, waiting for transfers between devices, shards(): lax.all_to_all(keys, 'dp', split_axis=0, concat_axis=1, tiled=True)  10.7 us
    all_to_all x1, waiting for transfers between devices, shards(): lax.all_to_all(grads, 'dp', split_axis=0, concat_axis=1, tiled=True)  10.2 us
  transfers between devices with their start and end apart: 16, of which 10 were waited for; matrix products, arithmetic and copies ran while one was open for 31% of the time, Pallas kernels for 0%

commit v1 on v0

v1 whole, which is shorter than its diff:
```python
import functools
import math

import jax
import jax.numpy as jnp
from jax import lax
from jax.experimental import pallas as pl
from jax.experimental.pallas import tpu as pltpu
from jax.sharding import PartitionSpec as P

HEAD = 128
N_DP = 64
N_MP = 8
N_Z = 16
N_Y = 4
ROWS = 8
CAP = N_DP * ROWS
SEQS = 64
PER = SEQS // N_MP
GROUP = 4
TILES = 1 + GROUP
CHUNKS = ((0, 2), (2, 3), (3, 4), (4, 5))
ROW_BLOCK = 256
MESH = pl.DeviceIdType.MESH
F32 = jnp.float32
BF16 = jnp.bfloat16


def dot_nt(a, b):
    return lax.dot_general(a, b, (((1,), (1,)), ((), ())), preferred_element_type=F32)


def dot_nn(a, b):
    return lax.dot_general(a, b, (((1,), (0,)), ((), ())), preferred_element_type=F32)


def dot_tn(a, b):
    return lax.dot_general(a, b, (((0,), (0,)), ((), ())), preferred_element_type=F32)


def kernel(
    flags, lengths, q_ref, k_ref, v_ref, g_ref,
    out_ref, dq_ref, dk_ref, dv_ref,
    pack, stage, full, k_buf, v_buf, dk_acc, dv_acc,
    send_a, recv_a, send_b, recv_b, *held,
):
    dp = lax.axis_index("dp")
    mp = lax.axis_index("mp")

    barrier = pltpu.get_barrier_semaphore()

    def greet_mp(step, carry):
        peer = lax.rem(mp + step, N_MP)
        pl.semaphore_signal(barrier, inc=1, device_id=(dp, peer), device_id_type=MESH)
        return carry

    def greet_dp(step, carry):
        peer = lax.rem(dp + step, N_DP)
        pl.semaphore_signal(barrier, inc=1, device_id=(peer, mp), device_id_type=MESH)
        return carry

    lax.fori_loop(1, N_MP, greet_mp, 0)
    lax.fori_loop(1, N_DP, greet_dp, 0)

    def columns(head):
        return pl.ds(pl.multiple_of(head * HEAD, HEAD), HEAD)

    def join(upper, lower):
        both = jnp.concatenate([upper.astype(F32), lower.astype(F32)], axis=1)
        return both.astype(BF16)

    def fill(h, carry):
        pack[h, 0] = join(k_ref[:, :, columns(h)], v_ref[:, :, columns(h)])
        for j in range(GROUP):
            cols = columns(h * GROUP + j)
            pack[h, 1 + j] = join(q_ref[:, :, cols], g_ref[:, :, cols])
        return carry

    lax.fori_loop(0, N_MP, fill, 0)
    pl.semaphore_wait(barrier, N_MP - 1 + N_DP - 1)

    mine = pl.ds(pl.multiple_of(mp * PER, PER), PER)
    for c, (lo, hi) in enumerate(CHUNKS):

        def send_heads(step, carry, c=c, lo=lo, hi=hi):
            peer = lax.rem(mp + step, N_MP)
            pltpu.make_async_remote_copy(
                src_ref=pack.at[peer, lo:hi],
                dst_ref=held[c].at[:, mine],
                send_sem=send_a.at[c],
                recv_sem=recv_a.at[c],
                device_id=(dp, peer),
                device_id_type=MESH,
            ).start()
            return carry

        lax.fori_loop(1, N_MP, send_heads, 0)
        for t in range(lo, hi):
            held[c][t - lo, mine] = pack[mp, t]

    def sequence_of(slot):
        one = jnp.where(flags[1, slot] == 1, slot ^ (N_DP // 4), slot)
        return jnp.where(flags[0, one] == 1, one ^ (N_DP // 2), one)

    def wait_all(sem, ref):
        pltpu.make_async_copy(ref, ref, sem).wait()

    y, z = dp // N_Z, lax.rem(dp, N_Z)
    my_sequence = sequence_of(dp)
    for c, (lo, hi) in enumerate(CHUNKS):
        wait_all(recv_a.at[c], held[c].at[:, 0 : SEQS - PER])
        for t in range(lo, hi):
            full[t, dp] = held[c][t - lo, my_sequence]

        def send_slot(step, carry, c=c, lo=lo, hi=hi):
            turn, dy = step // N_Y, lax.rem(step, N_Y)
            half = (turn + 1) // 2
            dz = jnp.where(lax.rem(turn, 2) == 1, half, N_Z - half)
            peer = lax.rem(y + dy, N_Y) * N_Z + lax.rem(z + dz, N_Z)
            sequence = sequence_of(peer)
            for t in range(lo, hi):
                stage[t, peer] = held[c][t - lo, sequence]
            pltpu.make_async_remote_copy(
                src_ref=stage.at[lo:hi, peer],
                dst_ref=full.at[lo:hi, dp],
                send_sem=send_b.at[c],
                recv_sem=recv_b.at[c],
                device_id=(peer, mp),
                device_id_type=MESH,
            ).start()
            return carry

        lax.fori_loop(1, N_DP, send_slot, 0)

    length = lengths[my_sequence]
    scale = 1.0 / math.sqrt(HEAD)
    live = lax.broadcasted_iota(jnp.int32, (CAP, 1), 0) < length

    def halves(t):
        both = full[t].astype(F32)
        return both[:, :ROWS].reshape(CAP, HEAD), both[:, ROWS:].reshape(CAP, HEAD)

    for c, (lo, hi) in enumerate(CHUNKS):
        wait_all(recv_b.at[c], full.at[lo:hi, 0 : N_DP - 1])
        for t in range(lo, hi):
            if t == 0:
                keys, values = halves(0)
                k_buf[...] = keys.astype(BF16)
                v_buf[...] = values.astype(BF16)
                continue
            j = t - 1
            q_all, g_all = halves(t)
            q_all = q_all.astype(BF16)
            g_all = jnp.where(live, g_all, 0.0).astype(BF16)
            for first in reversed(range(0, CAP, ROW_BLOCK)):
                last = first + ROW_BLOCK
                q, g = q_all[first:last], g_all[first:last]
                k, v = k_buf[:last], v_buf[:last]
                scores = dot_nt(q, k) * scale
                row = lax.broadcasted_iota(jnp.int32, (ROW_BLOCK, last), 0) + first
                col = lax.broadcasted_iota(jnp.int32, (ROW_BLOCK, last), 1)
                scores = jnp.where(col <= row, scores, -1e30)
                top = jnp.max(scores, axis=-1, keepdims=True)
                weights = jnp.exp(scores - top)
                weights = weights / jnp.sum(weights, axis=-1, keepdims=True)
                probs = weights.astype(BF16)
                out = jnp.where(live[first:last], dot_nn(probs, v), 0.0)
                dprob = dot_nt(g, v)
                delta = jnp.sum(weights * dprob, axis=-1, keepdims=True)
                dscore = (weights * (dprob - delta) * scale).astype(BF16)
                lanes = slice(j * HEAD, (j + 1) * HEAD)
                out_ref[0, first:last, lanes] = out.astype(BF16)
                dq_ref[0, first:last, lanes] = dot_nn(dscore, k).astype(BF16)
                dv_part = dot_tn(probs, g)
                dk_part = dot_tn(dscore, q)
                if j == 0 and last == CAP:
                    dv_acc[...] = dv_part
                    dk_acc[...] = dk_part
                else:
                    dv_acc[:last] += dv_part
                    dk_acc[:last] += dk_part
    dk_ref[0] = dk_acc[...].astype(BF16)
    dv_ref[0] = dv_acc[...].astype(BF16)
    for c, (lo, hi) in enumerate(CHUNKS):
        wait_all(send_a.at[c], held[c].at[:, 0 : SEQS - PER])
        wait_all(send_b.at[c], full.at[lo:hi, 0 : N_DP - 1])


def shards(q_gen, k_gen, v_gen, grad_gen, lengths, swap_flags):
    vmem = pl.BlockSpec(memory_space=pltpu.VMEM)
    smem = pl.BlockSpec(memory_space=pltpu.SMEM)
    wide = jax.ShapeDtypeStruct((1, CAP, GROUP * HEAD), BF16)
    narrow = jax.ShapeDtypeStruct((1, CAP, HEAD), BF16)
    chunks = len(CHUNKS)
    return tuple(
        pl.pallas_call(
            kernel,
            out_shape=(wide, wide, narrow, narrow),
            in_specs=[smem, smem, vmem, vmem, vmem, vmem],
            out_specs=(vmem, vmem, vmem, vmem),
            scratch_shapes=[
                pltpu.VMEM((N_MP, TILES, PER, 2 * ROWS, HEAD), BF16),
                pltpu.VMEM((TILES, N_DP, 2 * ROWS, HEAD), BF16),
                pltpu.VMEM((TILES, N_DP, 2 * ROWS, HEAD), BF16),
                pltpu.VMEM((CAP, HEAD), BF16),
                pltpu.VMEM((CAP, HEAD), BF16),
                pltpu.VMEM((CAP, HEAD), F32),
                pltpu.VMEM((CAP, HEAD), F32),
                pltpu.SemaphoreType.DMA((chunks,)),
                pltpu.SemaphoreType.DMA((chunks,)),
                pltpu.SemaphoreType.DMA((chunks,)),
                pltpu.SemaphoreType.DMA((chunks,)),
                *(pltpu.VMEM((hi - lo, SEQS, 2 * ROWS, HEAD), BF16) for lo, hi in CHUNKS),
            ],
            compiler_params=pltpu.CompilerParams(
                collective_id=0, has_side_effects=True, vmem_limit_bytes=40 * 2**20
            ),
        )(swap_flags, lengths, q_gen, k_gen, v_gen, grad_gen)
    )


def solution(mesh):
    rollout = P("mp", "dp", None)
    trainer = P("dp", None, "mp")
    return jax.shard_map(
        shards,
        mesh=mesh,
        in_specs=(rollout, rollout, rollout, rollout, P(), P()),
        out_specs=(trainer, trainer, trainer, trainer),
        check_vma=False,
    )
```

time: 302 us -> 100 us (0.33)
  the two profiles are of different devices: /device:TPU:40 before, /device:TPU:1 now
where the time goes in v1:
time: 100 us
  Pallas kernels  91.4 us (91%)
  local copies, waits for them, and re-layouts  8.11 us (8%)
    pallas_call x1, Pallas kernels, shards(): pl.pallas_call(kernel, out_shape=(wide, wide, narrow, narrow), in_specs=[...  91.4 us
    unnamed x16, local copies, waits for them, and re-layouts  8.11 us

profile of v1, /device:TPU:1, one launch (start us, length us, event | category | flops | bytes accessed | tf_op | source)
XLA Modules:
  0.0 100.2 jit_solution(12465252578813520178)
XLA Ops:
  0.6 0.0 copy-start
  0.6 1.0 %copy-done = bf16[8,8,4096]{2,1,0:T(8,128)(2,1)S(1)} copy-done((bf16[8,8,4096]{2,1,0:T(8,128)(2,1)S(1)}, bf16[8,8,4096]{2,1,0:T(8,128)(2,1)}, u32[]{:S(2)}) %copy-start) | copy-done | bytes 524312
  1.7 0.0 copy-start.1
  1.7 1.0 %copy-done.1 = bf16[8,8,4096]{2,1,0:T(8,128)(2,1)S(1)} copy-done((bf16[8,8,4096]{2,1,0:T(8,128)(2,1)S(1)}, bf16[8,8,4096]{2,1,0:T(8,128)(2,1)}, u32[]{:S(2)}) %copy-start.1) | copy-done | bytes 524312
  2.7 0.0 copy-start.2
  2.7 0.9 copy-done.2
  3.6 0.0 copy-start.3
  3.6 0.9 copy-done.3
  4.5 0.0 copy-start.4
  4.5 0.7 copy-done.4
  5.2 0.0 copy-start.5
  5.2 0.7 copy-done.5
  5.9 91.4 %shard_map.93 = (bf16[1,512,512]{2,1,0:T(8,128)(2,1)S(1)}, bf16[1,512,512]{2,1,0:T(8,128)(2,1)S(1)}, bf16[1,512,128]{2,1,0:T(8,128)(2,1)S(1)}, bf16[1,512,128]{2,1,0:T(8,128)(2,1)S(1)}) custom-call(s32[2,64]{1,0:T(2,128)S(1)} %copy-done.4, s32[64]{0:T(128)S(1)} %copy-done.5, bf16[8,8,4096]{2,1,0:T(8,128)(2,1)S(1)} %copy-done, ...), custom_call_target="tpu_custom_call" | custom-call | tf_op jit(solution)/shard_map/pallas_call | solution.py:196
  97.3 0.8 copy.14
  98.1 0.8 copy.15
  98.9 0.7 copy.16
  99.5 0.7 copy.17
Async XLA Ops:
  0.6 1.0 %copy-start = (bf16[8,8,4096]{2,1,0:T(8,128)(2,1)S(1)}, bf16[8,8,4096]{2,1,0:T(8,128)(2,1)}, u32[]{:S(2)}) copy-start(bf16[8,8,4096]{2,1,0:T(8,128)(2,1)} %q_ref.1) | copy-start | bytes 1572868
  1.7 1.0 %copy-start.1 = (bf16[8,8,4096]{2,1,0:T(8,128)(2,1)S(1)}, bf16[8,8,4096]{2,1,0:T(8,128)(2,1)}, u32[]{:S(2)}) copy-start(bf16[8,8,4096]{2,1,0:T(8,128)(2,1)} %g_ref.1) | copy-start | bytes 1572868
  2.7 0.9 copy-start.2
  3.6 0.9 copy-start.3
  4.5 0.7 copy-start.4
  5.2 0.7 copy-start.5

commit v2 on v1

--- a/solution.py
+++ b/solution.py
@@ -19,7 +19,7 @@
 PER = SEQS // N_MP
 GROUP = 4
 TILES = 1 + GROUP
-CHUNKS = ((0, 2), (2, 3), (3, 4), (4, 5))
+CHUNKS = ((0, 1), (1, 2), (2, 3), (3, 4), (4, 5))
 ROW_BLOCK = 256
 MESH = pl.DeviceIdType.MESH
 F32 = jnp.float32
@@ -39,15 +39,25 @@
 
 
 def kernel(
+    flags_hbm, lengths_hbm, q_hbm, k_hbm, v_hbm, g_hbm,
+    out_ref, dq_ref, dk_ref, dv_ref,
     flags, lengths, q_ref, k_ref, v_ref, g_ref,
-    out_ref, dq_ref, dk_ref, dv_ref,
     pack, stage, full, k_buf, v_buf, dk_acc, dv_acc,
-    send_a, recv_a, send_b, recv_b, *held,
+    load_sem, send_a, recv_a, send_b, recv_b, *held,
 ):
     dp = lax.axis_index("dp")
     mp = lax.axis_index("mp")
-
-    barrier = pltpu.get_barrier_semaphore()
+    y, z = dp // N_Z, lax.rem(dp, N_Z)
+
+    loads = [
+        pltpu.make_async_copy(src, dst, load_sem.at[n])
+        for n, (src, dst) in enumerate(
+            (
+                (k_hbm, k_ref), (v_hbm, v_ref), (q_hbm, q_ref), (g_hbm, g_ref),
+                (flags_hbm, flags), (lengths_hbm, lengths),
+            )
+        )
+    ]
 
     def greet_mp(step, carry):
         peer = lax.rem(mp + step, N_MP)
@@ -59,8 +69,11 @@
         pl.semaphore_signal(barrier, inc=1, device_id=(peer, mp), device_id_type=MESH)
         return carry
 
+    barrier = pltpu.get_barrier_semaphore()
+    for load in loads:
+        load.start()
+    lax.fori_loop(1, N_DP, greet_dp, 0)
     lax.fori_loop(1, N_MP, greet_mp, 0)
-    lax.fori_loop(1, N_DP, greet_dp, 0)
 
     def columns(head):
         return pl.ds(pl.multiple_of(head * HEAD, HEAD), HEAD)
@@ -69,14 +82,20 @@
         both = jnp.concatenate([upper.astype(F32), lower.astype(F32)], axis=1)
         return both.astype(BF16)
 
-    def fill(h, carry):
-        pack[h, 0] = join(k_ref[:, :, columns(h)], v_ref[:, :, columns(h)])
-        for j in range(GROUP):
-            cols = columns(h * GROUP + j)
-            pack[h, 1 + j] = join(q_ref[:, :, cols], g_ref[:, :, cols])
-        return carry
-
-    lax.fori_loop(0, N_MP, fill, 0)
+    def fill(t):
+        def fill_head(h, carry):
+            if t == 0:
+                pack[h, 0] = join(k_ref[:, :, columns(h)], v_ref[:, :, columns(h)])
+            else:
+                cols = columns(h * GROUP + t - 1)
+                pack[h, t] = join(q_ref[:, :, cols], g_ref[:, :, cols])
+            return carry
+
+        lax.fori_loop(0, N_MP, fill_head, 0)
+
+    loads[0].wait()
+    loads[1].wait()
+    fill(0)
     pl.semaphore_wait(barrier, N_MP - 1 + N_DP - 1)
 
     mine = pl.ds(pl.multiple_of(mp * PER, PER), PER)
@@ -94,6 +113,11 @@
             ).start()
             return carry
 
+        if c == 1:
+            for load in loads[2:]:
+                load.wait()
+        for t in range(max(lo, 1), hi):
+            fill(t)
         lax.fori_loop(1, N_MP, send_heads, 0)
         for t in range(lo, hi):
             held[c][t - lo, mine] = pack[mp, t]
@@ -105,7 +129,6 @@
     def wait_all(sem, ref):
         pltpu.make_async_copy(ref, ref, sem).wait()
 
-    y, z = dp // N_Z, lax.rem(dp, N_Z)
     my_sequence = sequence_of(dp)
     for c, (lo, hi) in enumerate(CHUNKS):
         wait_all(recv_a.at[c], held[c].at[:, 0 : SEQS - PER])
@@ -114,9 +137,13 @@
 
         def send_slot(step, carry, c=c, lo=lo, hi=hi):
             turn, dy = step // N_Y, lax.rem(step, N_Y)
-            half = (turn + 1) // 2
-            dz = jnp.where(lax.rem(turn, 2) == 1, half, N_Z - half)
-            peer = lax.rem(y + dy, N_Y) * N_Z + lax.rem(z + dz, N_Z)
+            j = (turn - 1) // 2
+            wrapped = jnp.maximum(z - 7, 0)
+            up = jnp.where(j < wrapped, j, jnp.where(wrapped == 0, z + 1 + j, N_Z - 1 - (j - wrapped)))
+            low = jnp.minimum(z, 7)
+            down = jnp.where(j < low, wrapped + j, N_Z - 1 - (j - low))
+            to_z = jnp.where(turn == 0, z, jnp.where(lax.rem(turn, 2) == 1, up, down))
+            peer = lax.rem(y + dy, N_Y) * N_Z + to_z
             sequence = sequence_of(peer)
             for t in range(lo, hi):
                 stage[t, peer] = held[c][t - lo, sequence]
@@ -186,36 +213,68 @@
         wait_all(send_b.at[c], full.at[lo:hi, 0 : N_DP - 1])
 
 
+def write_out(*refs):
+    sources, results, held, sem_in, sem_out = refs[:4], refs[4:8], refs[8:12], *refs[12:]
+    loads = [pltpu.make_async_copy(*pair, sem_in.at[n]) for n, pair in enumerate(zip(sources, held))]
+    stores = [pltpu.make_async_copy(*pair, sem_out.at[n]) for n, pair in enumerate(zip(held, results))]
+    for load in loads:
+        load.start()
+    for load, store in zip(loads, stores):
+        load.wait()
+        store.start()
+    for store in stores:
+        store.wait()
+
+
 def shards(q_gen, k_gen, v_gen, grad_gen, lengths, swap_flags):
     vmem = pl.BlockSpec(memory_space=pltpu.VMEM)
-    smem = pl.BlockSpec(memory_space=pltpu.SMEM)
+    hbm = pl.BlockSpec(memory_space=pl.ANY)
     wide = jax.ShapeDtypeStruct((1, CAP, GROUP * HEAD), BF16)
     narrow = jax.ShapeDtypeStruct((1, CAP, HEAD), BF16)
     chunks = len(CHUNKS)
+    results = pl.pallas_call(
+        kernel,
+        out_shape=(wide, wide, narrow, narrow),
+        in_specs=[hbm] * 6,
+        out_specs=(vmem, vmem, vmem, vmem),
+        scratch_shapes=[
+            pltpu.SMEM(swap_flags.shape, jnp.int32),
+            pltpu.SMEM(lengths.shape, jnp.int32),
+            pltpu.VMEM(q_gen.shape, BF16),
+            pltpu.VMEM(k_gen.shape, BF16),
+            pltpu.VMEM(v_gen.shape, BF16),
+            pltpu.VMEM(grad_gen.shape, BF16),
+            pltpu.VMEM((N_MP, TILES, PER, 2 * ROWS, HEAD), BF16),
+            pltpu.VMEM((TILES, N_DP, 2 * ROWS, HEAD), BF16),
+            pltpu.VMEM((TILES, N_DP, 2 * ROWS, HEAD), BF16),
+            pltpu.VMEM((CAP, HEAD), BF16),
+            pltpu.VMEM((CAP, HEAD), BF16),
+            pltpu.VMEM((CAP, HEAD), F32),
+            pltpu.VMEM((CAP, HEAD), F32),
+            pltpu.SemaphoreType.DMA((6,)),
+            pltpu.SemaphoreType.DMA((chunks,)),
+            pltpu.SemaphoreType.DMA((chunks,)),
+            pltpu.SemaphoreType.DMA((chunks,)),
+            pltpu.SemaphoreType.DMA((chunks,)),
+            *(pltpu.VMEM((hi - lo, SEQS, 2 * ROWS, HEAD), BF16) for lo, hi in CHUNKS),
+        ],
+        compiler_params=pltpu.CompilerParams(
+            collective_id=0, has_side_effects=True, vmem_limit_bytes=56 * 2**20
+        ),
+    )(swap_flags, lengths, q_gen, k_gen, v_gen, grad_gen)
     return tuple(
         pl.pallas_call(
-            kernel,
+            write_out,
             out_shape=(wide, wide, narrow, narrow),
-            in_specs=[smem, smem, vmem, vmem, vmem, vmem],
-            out_specs=(vmem, vmem, vmem, vmem),
+            in_specs=[hbm] * 4,
+            out_specs=(hbm, hbm, hbm, hbm),
             scratch_shapes=[
-                pltpu.VMEM((N_MP, TILES, PER, 2 * ROWS, HEAD), BF16),
-                pltpu.VMEM((TILES, N_DP, 2 * ROWS, HEAD), BF16),
-                pltpu.VMEM((TILES, N_DP, 2 * ROWS, HEAD), BF16),
-                pltpu.VMEM((CAP, HEAD), BF16),
-                pltpu.VMEM((CAP, HEAD), BF16),
-                pltpu.VMEM((CAP, HEAD), F32),
-                pltpu.VMEM((CAP, HEAD), F32),
-                pltpu.SemaphoreType.DMA((chunks,)),
-                pltpu.SemaphoreType.DMA((chunks,)),
-                pltpu.SemaphoreType.DMA((chunks,)),
-                pltpu.SemaphoreType.DMA((chunks,)),
-                *(pltpu.VMEM((hi - lo, SEQS, 2 * ROWS, HEAD), BF16) for lo, hi in CHUNKS),
+                *(pltpu.VMEM(result.shape, BF16) for result in (wide, wide, narrow, narrow)),
+                pltpu.SemaphoreType.DMA((4,)),
+                pltpu.SemaphoreType.DMA((4,)),
             ],
-            compiler_params=pltpu.CompilerParams(
-                collective_id=0, has_side_effects=True, vmem_limit_bytes=40 * 2**20
-            ),
-        )(swap_flags, lengths, q_gen, k_gen, v_gen, grad_gen)
+            compiler_params=pltpu.CompilerParams(vmem_limit_bytes=56 * 2**20),
+        )(*results)
     )
 
 

time: 100 us -> 87.1 us (0.87); the launches traced: 100 us -> 85.4 us
  local copies, waits for them, and re-layouts: 8.11 us -> 0 us
  Pallas kernels: 91.4 us -> 84.7 us
    pallas_call x1, Pallas kernels: 91.4 us -> 82.6 us  [shards(): pl.pallas_call(kernel, out_shape=(wide, wide, narrow, narrow), in_specs=[...]
    unnamed x16 -> x0, local copies, waits for them, and re-layouts: 8.11 us -> none
    pallas_call x0 -> x1, Pallas kernels: none -> 2.15 us  [shards(): pl.pallas_call(write_out, out_shape=(wide, wide, narrow, narrow), in_spec...]
where the time goes in v2:
time: 87.1 us; the launch traced here: 85.4 us
  Pallas kernels  84.7 us (97%)
    pallas_call x1, Pallas kernels, shards(): pl.pallas_call(kernel, out_shape=(wide, wide, narrow, narrow), in_specs=[...  82.6 us
    pallas_call x1, Pallas kernels, shards(): pl.pallas_call(write_out, out_shape=(wide, wide, narrow, narrow), in_spec...  2.15 us

profile of v2, /device:TPU:1, one launch (start us, length us, event | category | flops | bytes accessed | tf_op | source)
XLA Modules:
  0.0 85.4 jit_solution(15626951169860558585)
XLA Ops:
  0.6 82.6 %shard_map.93 = (bf16[1,512,512]{2,1,0:T(8,128)(2,1)}, bf16[1,512,512]{2,1,0:T(8,128)(2,1)}, bf16[1,512,128]{2,1,0:T(8,128)(2,1)}, bf16[1,512,128]{2,1,0:T(8,128)(2,1)}) custom-call(s32[2,64]{1,0:T(2,128)} %flags_hbm.1, s32[64]{0:T(128)} %lengths_hbm.1, bf16[8,8,4096]{2,1,0:T(8,128)(2,1)} %q_hbm.1, bf16[8,8,1024]{2,1,0:T(8,128)(2,1)} %k_hbm.1, ...), custom_call_target="tpu_custom_call" | custom-call | tf_op jit(solution)/shard_map/pallas_call | solution.py:235
  83.2 2.2 %shard_map.94 = (bf16[1,512,512]{2,1,0:T(8,128)(2,1)}, bf16[1,512,512]{2,1,0:T(8,128)(2,1)}, bf16[1,512,128]{2,1,0:T(8,128)(2,1)}, bf16[1,512,128]{2,1,0:T(8,128)(2,1)}) custom-call(bf16[1,512,512]{2,1,0:T(8,128)(2,1)} %get-tuple-element.8.refs_0_, bf16[1,512,512]{2,1,0:T(8,128)(2,1)} %get-tuple-element.9.refs_1_, ...), custom_call_target="tpu_custom_call" | custom-call | tf_op jit(solution)/shard_map/pallas_call | solution.py:266

commit v3 on v2

--- a/solution.py
+++ b/solution.py
@@ -19,7 +19,7 @@
 PER = SEQS // N_MP
 GROUP = 4
 TILES = 1 + GROUP
-CHUNKS = ((0, 1), (1, 2), (2, 3), (3, 4), (4, 5))
+CHUNKS = ((1, 2), (2, 3), (3, 4), (4, 5))
 ROW_BLOCK = 256
 MESH = pl.DeviceIdType.MESH
 F32 = jnp.float32
@@ -42,12 +42,14 @@
     flags_hbm, lengths_hbm, q_hbm, k_hbm, v_hbm, g_hbm,
     out_ref, dq_ref, dk_ref, dv_ref,
     flags, lengths, q_ref, k_ref, v_ref, g_ref,
-    pack, stage, full, k_buf, v_buf, dk_acc, dv_acc,
-    load_sem, send_a, recv_a, send_b, recv_b, *held,
+    pack, pack_kv, by_z, by_x, by_y, stage, full, k_buf, v_buf, dk_acc, dv_acc,
+    load_sem, send_kv, recv_kv, send_a, recv_a, send_b, recv_b, *held,
 ):
     dp = lax.axis_index("dp")
     mp = lax.axis_index("mp")
     y, z = dp // N_Z, lax.rem(dp, N_Z)
+    x, core = mp // 2, lax.rem(mp, 2)
+    hub = core == z // PER
 
     loads = [
         pltpu.make_async_copy(src, dst, load_sem.at[n])
@@ -84,19 +86,45 @@
 
     def fill(t):
         def fill_head(h, carry):
-            if t == 0:
-                pack[h, 0] = join(k_ref[:, :, columns(h)], v_ref[:, :, columns(h)])
-            else:
-                cols = columns(h * GROUP + t - 1)
-                pack[h, t] = join(q_ref[:, :, cols], g_ref[:, :, cols])
+            cols = columns(h * GROUP + t - 1)
+            pack[h, t - 1] = join(q_ref[:, :, cols], g_ref[:, :, cols])
             return carry
 
         lax.fori_loop(0, N_MP, fill_head, 0)
+
+    def fill_kv(h, carry):
+        pack_kv[:, h] = join(k_ref[:, :, columns(h)], v_ref[:, :, columns(h)])
+        return carry
+
+    def remote(src, dst, send, recv, device):
+        pltpu.make_async_remote_copy(
+            src_ref=src, dst_ref=dst, send_sem=send, recv_sem=recv, device_id=device, device_id_type=MESH
+        ).start()
+
+    def wait_all(sem, ref):
+        pltpu.make_async_copy(ref, ref, sem).wait()
 
     loads[0].wait()
     loads[1].wait()
-    fill(0)
+    lax.fori_loop(0, N_MP, fill_kv, 0)
     pl.semaphore_wait(barrier, N_MP - 1 + N_DP - 1)
+
+    own = lax.rem(z, PER)
+
+    def send_kv_z(step, carry):
+        i = lax.rem(own + step, PER)
+        remote(pack_kv.at[i], by_z.at[z], send_kv.at[0], recv_kv.at[0], (y * N_Z + core * PER + i, mp))
+        return carry
+
+    lax.fori_loop(1, PER, send_kv_z, 0)
+
+    @pl.when(hub)
+    def _():
+        by_z[z] = pack_kv[own]
+
+    @pl.when(jnp.logical_not(hub))
+    def _():
+        send_kv_z(0, 0)
 
     mine = pl.ds(pl.multiple_of(mp * PER, PER), PER)
     for c, (lo, hi) in enumerate(CHUNKS):
@@ -104,7 +132,7 @@
         def send_heads(step, carry, c=c, lo=lo, hi=hi):
             peer = lax.rem(mp + step, N_MP)
             pltpu.make_async_remote_copy(
-                src_ref=pack.at[peer, lo:hi],
+                src_ref=pack.at[peer, lo - 1 : hi - 1],
                 dst_ref=held[c].at[:, mine],
                 send_sem=send_a.at[c],
                 recv_sem=recv_a.at[c],
@@ -113,21 +141,51 @@
             ).start()
             return carry
 
-        if c == 1:
+        if c == 0:
             for load in loads[2:]:
                 load.wait()
-        for t in range(max(lo, 1), hi):
+        for t in range(lo, hi):
             fill(t)
         lax.fori_loop(1, N_MP, send_heads, 0)
         for t in range(lo, hi):
-            held[c][t - lo, mine] = pack[mp, t]
+            held[c][t - lo, mine] = pack[mp, t - 1]
 
     def sequence_of(slot):
         one = jnp.where(flags[1, slot] == 1, slot ^ (N_DP // 4), slot)
         return jnp.where(flags[0, one] == 1, one ^ (N_DP // 2), one)
 
-    def wait_all(sem, ref):
-        pltpu.make_async_copy(ref, ref, sem).wait()
+    def send_kv_x():
+        @pl.when(hub)
+        def _():
+            wait_all(recv_kv.at[0], by_z.at[0 : N_Z - 1])
+
+            def send(step, carry):
+                peer = lax.rem(mp + step, N_MP)
+                remote(by_z.at[:, peer], by_x.at[x], send_kv.at[1], recv_kv.at[1], (dp, peer))
+                return carry
+
+            lax.fori_loop(1, N_MP, send, 0)
+            by_x[x] = by_z[:, mp]
+
+    def send_kv_y():
+        @pl.when(hub)
+        def _():
+            wait_all(recv_kv.at[1], by_x.at[0 : N_Y - 1])
+
+        @pl.when(jnp.logical_not(hub))
+        def _():
+            wait_all(recv_kv.at[1], by_x)
+
+        def send(step, carry):
+            to_y = lax.rem(y + step, N_Y)
+            slot = to_y * N_Z + z
+            by_y[to_y] = by_x[sequence_of(slot) // N_Z]
+            remote(by_y.at[to_y], full.at[0, from_here], send_kv.at[2], recv_kv.at[2], (slot, mp))
+            return carry
+
+        from_here = pl.ds(pl.multiple_of(y * N_Z, N_Z), N_Z)
+        lax.fori_loop(1, N_Y, send, 0)
+        full[0, from_here] = by_x[my_sequence // N_Z]
 
     my_sequence = sequence_of(dp)
     for c, (lo, hi) in enumerate(CHUNKS):
@@ -146,9 +204,9 @@
             peer = lax.rem(y + dy, N_Y) * N_Z + to_z
             sequence = sequence_of(peer)
             for t in range(lo, hi):
-                stage[t, peer] = held[c][t - lo, sequence]
+                stage[t - 1, peer] = held[c][t - lo, sequence]
             pltpu.make_async_remote_copy(
-                src_ref=stage.at[lo:hi, peer],
+                src_ref=stage.at[lo - 1 : hi - 1, peer],
                 dst_ref=full.at[lo:hi, dp],
                 send_sem=send_b.at[c],
                 recv_sem=recv_b.at[c],
@@ -158,6 +216,10 @@
             return carry
 
         lax.fori_loop(1, N_DP, send_slot, 0)
+        if c == 0:
+            send_kv_x()
+        if c == 1:
+            send_kv_y()
 
     length = lengths[my_sequence]
     scale = 1.0 / math.sqrt(HEAD)
@@ -167,14 +229,13 @@
         both = full[t].astype(F32)
         return both[:, :ROWS].reshape(CAP, HEAD), both[:, ROWS:].reshape(CAP, HEAD)
 
+    wait_all(recv_kv.at[2], full.at[0, 0 : N_DP - N_Z])
+    keys, values = halves(0)
+    k_buf[...] = keys.astype(BF16)
+    v_buf[...] = values.astype(BF16)
     for c, (lo, hi) in enumerate(CHUNKS):
         wait_all(recv_b.at[c], full.at[lo:hi, 0 : N_DP - 1])
         for t in range(lo, hi):
-            if t == 0:
-                keys, values = halves(0)
-                k_buf[...] = keys.astype(BF16)
-                v_buf[...] = values.astype(BF16)
-                continue
             j = t - 1
             q_all, g_all = halves(t)
             q_all = q_all.astype(BF16)
@@ -208,6 +269,16 @@
                     dk_acc[:last] += dk_part
     dk_ref[0] = dk_acc[...].astype(BF16)
     dv_ref[0] = dv_acc[...].astype(BF16)
+    @pl.when(hub)
+    def _():
+        wait_all(send_kv.at[0], pack_kv.at[0 : PER - 1])
+        wait_all(send_kv.at[1], by_z.at[:, 0 : N_MP - 1])
+
+    @pl.when(jnp.logical_not(hub))
+    def _():
+        wait_all(send_kv.at[0], pack_kv)
+
+    wait_all(send_kv.at[2], full.at[0, 0 : N_DP - N_Z])
     for c, (lo, hi) in enumerate(CHUNKS):
         wait_all(send_a.at[c], held[c].at[:, 0 : SEQS - PER])
         wait_all(send_b.at[c], full.at[lo:hi, 0 : N_DP - 1])
@@ -244,14 +315,20 @@
             pltpu.VMEM(k_gen.shape, BF16),
             pltpu.VMEM(v_gen.shape, BF16),
             pltpu.VMEM(grad_gen.shape, BF16),
-            pltpu.VMEM((N_MP, TILES, PER, 2 * ROWS, HEAD), BF16),
-            pltpu.VMEM((TILES, N_DP, 2 * ROWS, HEAD), BF16),
+            pltpu.VMEM((N_MP, GROUP, PER, 2 * ROWS, HEAD), BF16),
+            pltpu.VMEM((PER, N_MP, 2 * ROWS, HEAD), BF16),
+            pltpu.VMEM((N_Z, N_MP, 2 * ROWS, HEAD), BF16),
+            pltpu.VMEM((N_Y, N_Z, 2 * ROWS, HEAD), BF16),
+            pltpu.VMEM((N_Y, N_Z, 2 * ROWS, HEAD), BF16),
+            pltpu.VMEM((GROUP, N_DP, 2 * ROWS, HEAD), BF16),
             pltpu.VMEM((TILES, N_DP, 2 * ROWS, HEAD), BF16),
             pltpu.VMEM((CAP, HEAD), BF16),
             pltpu.VMEM((CAP, HEAD), BF16),
             pltpu.VMEM((CAP, HEAD), F32),
             pltpu.VMEM((CAP, HEAD), F32),
             pltpu.SemaphoreType.DMA((6,)),
+            pltpu.SemaphoreType.DMA((3,)),
+            pltpu.SemaphoreType.DMA((3,)),
             pltpu.SemaphoreType.DMA((chunks,)),
             pltpu.SemaphoreType.DMA((chunks,)),
             pltpu.SemaphoreType.DMA((chunks,)),

time: 87.1 us -> 83 us (0.953)
  the two profiles are of different devices: /device:TPU:1 before, /device:TPU:36 now
where the time goes in v3:
time: 83 us; the launch traced here: 82.9 us
  Pallas kernels  82.2 us (99%)
    pallas_call x1, Pallas kernels, shards(): pl.pallas_call(kernel, out_shape=(wide, wide, narrow, narrow), in_specs=[...  80.1 us
    pallas_call x1, Pallas kernels, shards(): pl.pallas_call(write_out, out_shape=(wide, wide, narrow, narrow), in_spec...  2.15 us

profile of v3, /device:TPU:36, one launch (start us, length us, event | category | flops | bytes accessed | tf_op | source)
XLA Modules:
  0.0 82.9 jit_solution(15408118819977350501)
XLA Ops:
  0.6 80.1 %shard_map.93 = (bf16[1,512,512]{2,1,0:T(8,128)(2,1)}, bf16[1,512,512]{2,1,0:T(8,128)(2,1)}, bf16[1,512,128]{2,1,0:T(8,128)(2,1)}, bf16[1,512,128]{2,1,0:T(8,128)(2,1)}) custom-call(s32[2,64]{1,0:T(2,128)} %flags_hbm.1, s32[64]{0:T(128)} %lengths_hbm.1, bf16[8,8,4096]{2,1,0:T(8,128)(2,1)} %q_hbm.1, bf16[8,8,1024]{2,1,0:T(8,128)(2,1)} %k_hbm.1, ...), custom_call_target="tpu_custom_call" | custom-call | tf_op jit(solution)/shard_map/pallas_call | solution.py:306
  80.7 2.2 %shard_map.94 = (bf16[1,512,512]{2,1,0:T(8,128)(2,1)}, bf16[1,512,512]{2,1,0:T(8,128)(2,1)}, bf16[1,512,128]{2,1,0:T(8,128)(2,1)}, bf16[1,512,128]{2,1,0:T(8,128)(2,1)}) custom-call(bf16[1,512,512]{2,1,0:T(8,128)(2,1)} %get-tuple-element.8.refs_0_, bf16[1,512,512]{2,1,0:T(8,128)(2,1)} %get-tuple-element.9.refs_1_, ...), custom_call_target="tpu_custom_call" | custom-call | tf_op jit(solution)/shard_map/pallas_call | solution.py:343

commit v4 on v3

--- a/solution.py
+++ b/solution.py
@@ -20,7 +20,7 @@
 GROUP = 4
 TILES = 1 + GROUP
 CHUNKS = ((1, 2), (2, 3), (3, 4), (4, 5))
-ROW_BLOCK = 256
+ROW_BLOCK = 512
 MESH = pl.DeviceIdType.MESH
 F32 = jnp.float32
 BF16 = jnp.bfloat16
@@ -216,9 +216,9 @@
             return carry
 
         lax.fori_loop(1, N_DP, send_slot, 0)
-        if c == 0:
+        if c == 1:
             send_kv_x()
-        if c == 1:
+        if c == 2:
             send_kv_y()
 
     length = lengths[my_sequence]
@@ -244,13 +244,13 @@
                 last = first + ROW_BLOCK
                 q, g = q_all[first:last], g_all[first:last]
                 k, v = k_buf[:last], v_buf[:last]
-                scores = dot_nt(q, k) * scale
+                scores = dot_nt(q, k)
                 row = lax.broadcasted_iota(jnp.int32, (ROW_BLOCK, last), 0) + first
                 col = lax.broadcasted_iota(jnp.int32, (ROW_BLOCK, last), 1)
                 scores = jnp.where(col <= row, scores, -1e30)
                 top = jnp.max(scores, axis=-1, keepdims=True)
-                weights = jnp.exp(scores - top)
-                weights = weights / jnp.sum(weights, axis=-1, keepdims=True)
+                weights = jnp.exp2((scores - top) * (scale * math.log2(math.e)))
+                weights = weights * (1.0 / jnp.sum(weights, axis=-1, keepdims=True))
                 probs = weights.astype(BF16)
                 out = jnp.where(live[first:last], dot_nn(probs, v), 0.0)
                 dprob = dot_nt(g, v)
@@ -285,16 +285,12 @@
 
 
 def write_out(*refs):
-    sources, results, held, sem_in, sem_out = refs[:4], refs[4:8], refs[8:12], *refs[12:]
-    loads = [pltpu.make_async_copy(*pair, sem_in.at[n]) for n, pair in enumerate(zip(sources, held))]
-    stores = [pltpu.make_async_copy(*pair, sem_out.at[n]) for n, pair in enumerate(zip(held, results))]
-    for load in loads:
-        load.start()
-    for load, store in zip(loads, stores):
-        load.wait()
-        store.start()
-    for store in stores:
-        store.wait()
+    sources, results, sem = refs[:4], refs[4:8], refs[8]
+    copies = [pltpu.make_async_copy(*pair, sem.at[n]) for n, pair in enumerate(zip(sources, results))]
+    for copy in copies:
+        copy.start()
+    for copy in copies:
+        copy.wait()
 
 
 def shards(q_gen, k_gen, v_gen, grad_gen, lengths, swap_flags):
@@ -305,7 +301,7 @@
     chunks = len(CHUNKS)
     results = pl.pallas_call(
         kernel,
-        out_shape=(wide, wide, narrow, narrow),
+        out_shape=tuple(pltpu.VMEM(r.shape, BF16) for r in (wide, wide, narrow, narrow)),
         in_specs=[hbm] * 6,
         out_specs=(vmem, vmem, vmem, vmem),
         scratch_shapes=[
@@ -343,14 +339,12 @@
         pl.pallas_call(
             write_out,
             out_shape=(wide, wide, narrow, narrow),
-            in_specs=[hbm] * 4,
+            in_specs=[vmem] * 4,
             out_specs=(hbm, hbm, hbm, hbm),
             scratch_shapes=[
-                *(pltpu.VMEM(result.shape, BF16) for result in (wide, wide, narrow, narrow)),
-                pltpu.SemaphoreType.DMA((4,)),
                 pltpu.SemaphoreType.DMA((4,)),
             ],
-            compiler_params=pltpu.CompilerParams(vmem_limit_bytes=56 * 2**20),
+            compiler_params=pltpu.CompilerParams(vmem_limit_bytes=2 * 2**20),
         )(*results)
     )
 

time: 83 us -> 80.2 us (0.966)
  the two profiles are of different devices: /device:TPU:36 before, /device:TPU:34 now
where the time goes in v4:
time: 80.2 us; the launch traced here: 80.1 us
  Pallas kernels  79.5 us (99%)
    pallas_call x1, Pallas kernels, shards(): pl.pallas_call(kernel, out_shape=tuple((pltpu.VMEM(r.shape, BF16) for r i...  78.4 us

profile of v4, /device:TPU:34, one launch (start us, length us, event | category | flops | bytes accessed | tf_op | source)
XLA Modules:
  0.0 80.1 jit_solution(11074006818400028249)
XLA Ops:
  0.6 78.4 %shard_map.93 = (bf16[1,512,512]{2,1,0:T(8,128)(2,1)S(1)}, bf16[1,512,512]{2,1,0:T(8,128)(2,1)S(1)}, bf16[1,512,128]{2,1,0:T(8,128)(2,1)S(1)}, bf16[1,512,128]{2,1,0:T(8,128)(2,1)S(1)}) custom-call(s32[2,64]{1,0:T(2,128)} %flags_hbm.1, s32[64]{0:T(128)} %lengths_hbm.1, bf16[8,8,4096]{2,1,0:T(8,128)(2,1)} %q_hbm.1, bf16[8,8,1024]{2,1,0:T(8,128)(2,1)} %k_hbm.1, ...), custom_call_target="tpu_custom_call" | custom-call | tf_op jit(solution)/shard_map/pallas_call | solution.py:302
  79.0 1.1 %shard_map.94 = (bf16[1,512,512]{2,1,0:T(8,128)(2,1)}, bf16[1,512,512]{2,1,0:T(8,128)(2,1)}, bf16[1,512,128]{2,1,0:T(8,128)(2,1)}, bf16[1,512,128]{2,1,0:T(8,128)(2,1)}) custom-call(bf16[1,512,512]{2,1,0:T(8,128)(2,1)S(1)} %get-tuple-element.8.refs_0_, bf16[1,512,512]{2,1,0:T(8,128)(2,1)S(1)} %get-tuple-element.9.refs_1_, ...), custom_call_target="tpu_custom_call" | custom-call | tf_op jit(solution)/shard_map/pallas_call | solution.py:339

commit v5 on v4

--- a/solution.py
+++ b/solution.py
@@ -188,10 +188,8 @@
         full[0, from_here] = by_x[my_sequence // N_Z]
 
     my_sequence = sequence_of(dp)
+    senders = []
     for c, (lo, hi) in enumerate(CHUNKS):
-        wait_all(recv_a.at[c], held[c].at[:, 0 : SEQS - PER])
-        for t in range(lo, hi):
-            full[t, dp] = held[c][t - lo, my_sequence]
 
         def send_slot(step, carry, c=c, lo=lo, hi=hi):
             turn, dy = step // N_Y, lax.rem(step, N_Y)
@@ -215,11 +213,27 @@
             ).start()
             return carry
 
-        lax.fori_loop(1, N_DP, send_slot, 0)
-        if c == 1:
-            send_kv_x()
-        if c == 2:
-            send_kv_y()
+        senders.append(send_slot)
+
+    def take(c):
+        lo, hi = CHUNKS[c]
+        wait_all(recv_a.at[c], held[c].at[:, 0 : SEQS - PER])
+        for t in range(lo, hi):
+            full[t, dp] = held[c][t - lo, my_sequence]
+
+    take(0)
+    lax.fori_loop(1, N_DP, senders[0], 0)
+    take(1)
+    lax.fori_loop(1, N_DP, senders[1], 0)
+    send_kv_x()
+    take(2)
+    take(3)
+    turn_at = jnp.where(z >= N_Z // 2, N_DP // 2, N_DP)
+    lax.fori_loop(1, turn_at, senders[2], 0)
+    lax.fori_loop(1, turn_at, senders[3], 0)
+    send_kv_y()
+    lax.fori_loop(turn_at, N_DP, senders[2], 0)
+    lax.fori_loop(turn_at, N_DP, senders[3], 0)
 
     length = lengths[my_sequence]
     scale = 1.0 / math.sqrt(HEAD)

time: 80.2 us -> 79.3 us (0.989)
  the two profiles are of different devices: /device:TPU:34 before, /device:TPU:132 now
where the time goes in v5:
time: 79.3 us; the launch traced here: 79.2 us
  Pallas kernels  78.5 us (99%)
    pallas_call x1, Pallas kernels, shards(): pl.pallas_call(kernel, out_shape=tuple((pltpu.VMEM(r.shape, BF16) for r i...  77.4 us

profile of v5, /device:TPU:132, one launch (start us, length us, event | category | flops | bytes accessed | tf_op | source)
XLA Modules:
  0.0 79.2 jit_solution(12010081351486146688)
XLA Ops:
  0.6 77.4 %shard_map.93 = (bf16[1,512,512]{2,1,0:T(8,128)(2,1)S(1)}, bf16[1,512,512]{2,1,0:T(8,128)(2,1)S(1)}, bf16[1,512,128]{2,1,0:T(8,128)(2,1)S(1)}, bf16[1,512,128]{2,1,0:T(8,128)(2,1)S(1)}) custom-call(s32[2,64]{1,0:T(2,128)} %flags_hbm.1, s32[64]{0:T(128)} %lengths_hbm.1, bf16[8,8,4096]{2,1,0:T(8,128)(2,1)} %q_hbm.1, bf16[8,8,1024]{2,1,0:T(8,128)(2,1)} %k_hbm.1, ...), custom_call_target="tpu_custom_call" | custom-call | tf_op jit(solution)/shard_map/pallas_call | solution.py:316
  78.1 1.1 %shard_map.94 = (bf16[1,512,512]{2,1,0:T(8,128)(2,1)}, bf16[1,512,512]{2,1,0:T(8,128)(2,1)}, bf16[1,512,128]{2,1,0:T(8,128)(2,1)}, bf16[1,512,128]{2,1,0:T(8,128)(2,1)}) custom-call(bf16[1,512,512]{2,1,0:T(8,128)(2,1)S(1)} %get-tuple-element.8.refs_0_, bf16[1,512,512]{2,1,0:T(8,128)(2,1)S(1)} %get-tuple-element.9.refs_1_, ...), custom_call_target="tpu_custom_call" | custom-call | tf_op jit(solution)/shard_map/pallas_call | solution.py:353

commit v6 on v5

--- a/solution.py
+++ b/solution.py
@@ -74,8 +74,8 @@
     barrier = pltpu.get_barrier_semaphore()
     for load in loads:
         load.start()
-    lax.fori_loop(1, N_DP, greet_dp, 0)
-    lax.fori_loop(1, N_MP, greet_mp, 0)
+    lax.fori_loop(1, N_DP, greet_dp, 0, unroll=True)
+    lax.fori_loop(1, N_MP, greet_mp, 0, unroll=True)
 
     def columns(head):
         return pl.ds(pl.multiple_of(head * HEAD, HEAD), HEAD)
@@ -228,7 +228,7 @@
     send_kv_x()
     take(2)
     take(3)
-    turn_at = jnp.where(z >= N_Z // 2, N_DP // 2, N_DP)
+    turn_at = jnp.where((z >= N_Z // 2) | (core == 0), N_DP // 2, N_DP)
     lax.fori_loop(1, turn_at, senders[2], 0)
     lax.fori_loop(1, turn_at, senders[3], 0)
     send_kv_y()

time: 79.3 us -> 79 us (level)
  the two profiles are of different devices: /device:TPU:132 before, /device:TPU:134 now
where the time goes in v6:
time: 79 us; the launch traced here: 78.8 us
  Pallas kernels  78.2 us (99%)
    pallas_call x1, Pallas kernels, shards(): pl.pallas_call(kernel, out_shape=tuple((pltpu.VMEM(r.shape, BF16) for r i...  77.1 us

profile of v6, /device:TPU:134, one launch (start us, length us, event | category | flops | bytes accessed | tf_op | source)
XLA Modules:
  0.0 78.8 jit_solution(15471113873196888343)
XLA Ops:
  0.6 77.1 %shard_map.93 = (bf16[1,512,512]{2,1,0:T(8,128)(2,1)S(1)}, bf16[1,512,512]{2,1,0:T(8,128)(2,1)S(1)}, bf16[1,512,128]{2,1,0:T(8,128)(2,1)S(1)}, bf16[1,512,128]{2,1,0:T(8,128)(2,1)S(1)}) custom-call(s32[2,64]{1,0:T(2,128)} %flags_hbm.1, s32[64]{0:T(128)} %lengths_hbm.1, bf16[8,8,4096]{2,1,0:T(8,128)(2,1)} %q_hbm.1, bf16[8,8,1024]{2,1,0:T(8,128)(2,1)} %k_hbm.1, ...), custom_call_target="tpu_custom_call" | custom-call | tf_op jit(solution)/shard_map/pallas_call | solution.py:316
  77.7 1.1 %shard_map.94 = (bf16[1,512,512]{2,1,0:T(8,128)(2,1)}, bf16[1,512,512]{2,1,0:T(8,128)(2,1)}, bf16[1,512,128]{2,1,0:T(8,128)(2,1)}, bf16[1,512,128]{2,1,0:T(8,128)(2,1)}) custom-call(bf16[1,512,512]{2,1,0:T(8,128)(2,1)S(1)} %get-tuple-element.8.refs_0_, bf16[1,512,512]{2,1,0:T(8,128)(2,1)S(1)} %get-tuple-element.9.refs_1_, ...), custom_call_target="tpu_custom_call" | custom-call | tf_op jit(solution)/shard_map/pallas_call | solution.py:353
